TPU v7x, 32 devices: a whole 2x2x4 slice. The times are simulated.
32 devices in a mesh: blk: 8 (over z, y), group: 4 (over x, core).
Axes of the slice: x: 2, y: 2, z: 4, core: 2. Of those that a mesh axis runs over, the one named last changes fastest.
Arguments:
- image_feats: float32 [2048, 768], P(('blk', 'group')), may hold values from -2 to 2
- text_feats: float32 [2048, 768], P(('blk', 'group')), may hold values from -2 to 2
- logit_scale: float32 [1], replicated, may hold values from 30 to 100
Outputs:
- image_grad: float32 [2048, 768], P(('blk', 'group'))
- text_grad: float32 [2048, 768], P(('blk', 'group'))
- mean_loss: float32 [1], replicated
- scale_grad: float32 [1], replicated
All inputs are finite; a program needn't handle non-finite values.
Results may differ from a plain program's by a relative error of at most 0.0003.
Values sent between devices are 32-bit elements; how exact they have to be, the bound alone decides.
A program may use at most 64 MiB of HBM per device.

v0:
```python
import jax
import jax.numpy as jnp
from jax import lax
from jax.sharding import PartitionSpec as P


def combined_all(x, axis, combine):
    everything = jax.tree.map(lambda part: lax.all_gather(part, axis), x)
    initial = jax.tree.map(lambda part: part[0], everything)

    def lap(k, so_far):
        return combine(so_far, jax.tree.map(lambda part: part[k], everything))

    return lax.fori_loop(1, lax.axis_size(axis), lap, initial)


def scores_of(scale, pieces, texts):
    return scale * lax.dot_general(
        pieces, texts, (((1,), (1,)), ((), ())), precision=lax.Precision.HIGHEST
    )


def combine_stats(first, second):
    top = jnp.maximum(first[0], second[0])
    return (top, first[1] * jnp.exp(first[0] - top) + second[1] * jnp.exp(second[0] - top))


def body(image_feats, text_feats, logit_scale):
    scale = logit_scale[0]
    rows = image_feats.shape[0]
    texts = lax.all_gather(text_feats, "group", axis=0, tiled=True)
    image_total = rows * lax.axis_size("blk")
    image_offset = lax.axis_index("blk") * rows
    text_offset = lax.axis_index("group") * rows
    fold_forward = lambda fn, init: fn(
        init, lax.all_gather(image_feats, "blk", axis=0, tiled=True), jnp.int32(0)
    )
    merge_rows = lambda stats: combined_all(stats, "blk", combine_stats)
    merge_columns = lambda stats: combined_all(stats, "group", combine_stats)
    fold_backward = lambda fn, init: fn(
        init, lax.all_gather(image_feats, "blk", axis=0, tiled=True), jnp.int32(0)
    )
    reduce_images = lambda partial_sum: lax.psum_scatter(
        partial_sum, "blk", scatter_dimension=0, tiled=True
    )
    reduce_texts = lambda partial_sum: lax.psum_scatter(
        partial_sum, "group", scatter_dimension=0, tiled=True
    )
    text_total = texts.shape[0]

    def forward(carry, pieces, start):
        row_top, row_total, column_top, column_total, stored = carry
        scores = scores_of(scale, pieces, texts)
        piece_top = jnp.max(scores, axis=1)
        piece_total = jnp.sum(jnp.exp(scores - piece_top[:, None]), axis=1)
        row_top = piece_top
        row_total = piece_total
        new_top = jnp.maximum(column_top, jnp.max(scores, axis=0))
        column_total = jnp.sum(jnp.exp(scores - new_top[None, :]), axis=0)
        return (row_top, row_total, new_top, column_total, stored)

    empty_store = jnp.zeros((), jnp.float32)
    initial = (
        jnp.full((image_total,), -1e30, jnp.float32),
        jnp.zeros((image_total,), jnp.float32),
        jnp.full((text_total,), -1e30, jnp.float32),
        jnp.zeros((text_total,), jnp.float32),
        empty_store,
    )
    row_top, row_total, column_top, column_total, stored = fold_forward(forward, initial)
    row_top, row_total = merge_rows((row_top, row_total))
    column_top, column_total = merge_columns((column_top, column_total))
    row_lse = row_top + jnp.log(row_total)
    column_lse = column_top + jnp.log(column_total)

    def backward(carry, pieces, start):
        image_part, text_part, weighted = carry
        scores = scores_of(scale, pieces, texts)
        weights = 0.5 * (jnp.exp(scores - row_lse[:, None]) + jnp.exp(scores - column_lse[None, :]))
        image_piece = scale * jnp.dot(weights, texts, precision=lax.Precision.HIGHEST)
        image_part = lax.dynamic_update_slice_in_dim(image_part, image_piece, start, 0)
        text_part = text_part + scale * lax.dot_general(
            weights, pieces, (((0,), (0,)), ((), ())), precision=lax.Precision.HIGHEST
        )
        return (image_part, text_part, weighted + jnp.sum(weights * scores))

    begin = (
        jnp.zeros((image_total, image_feats.shape[1]), jnp.float32),
        jnp.zeros((text_total, text_feats.shape[1]), jnp.float32),
        jnp.zeros((), jnp.float32),
    )
    image_part, text_part, weighted = fold_backward(backward, begin)
    image_grad = reduce_images(image_part) - scale * text_feats
    text_grad = reduce_texts(text_part) - scale * image_feats
    diagonal = scale * jnp.sum(image_feats * text_feats, axis=1)
    own_rows = lax.dynamic_slice_in_dim(row_lse, image_offset, rows)
    own_columns = lax.dynamic_slice_in_dim(column_lse, text_offset, rows)
    loss_part = 0.5 * jnp.sum(own_rows) + 0.5 * jnp.sum(own_columns) - jnp.sum(diagonal)
    scale_part = weighted - jnp.sum(diagonal)
    loss_total, scale_total = lax.psum((loss_part, scale_part), ("blk", "group"))
    batch = rows * lax.axis_size("blk") * lax.axis_size("group")
    mean_loss = jnp.reshape(loss_total / batch, (1,))
    scale_grad = jnp.reshape(scale_total / (scale * batch), (1,))
    return (image_grad, text_grad, mean_loss, scale_grad)


def solution(mesh):
    return jax.shard_map(
        body,
        mesh=mesh,
        in_specs=(P(("blk", "group"), None), P(("blk", "group"), None), P()),
        out_specs=(P(("blk", "group"), None), P(("blk", "group"), None), P(), P()),
        check_vma=False,
    )
```

profile of v0, /device:TPU:0, one launch (start us, length us, event | category | flops | bytes accessed | tf_op | source)
XLA Modules:
  0.0 269.4 jit_solution(12595510853168128930)
XLA Ops:
  7.2 0.0 all-gather.10.cloned.1.call-start
  7.2 0.7 all-gather.10.cloned.1.call-update
  7.9 0.0 reduce-scatter.5.cloned.1.call-start
  8.6 10.3 %all_gather.30 = f32[256,768]{1,0:T(8,128)S(1)} all-gather(f32[64,768]{1,0:T(8,128)} %param.8), channel_id=1, replica_groups=mesh['blk'=8,'group'=4] {'group'}, dimensions={0}, use_global_device_ids=true | all-gather | bytes 983040 | tf_op jit(solution)/shard_map/all_gather | solution.py:31
  18.8 38.3 %all-gather.10.cloned.1.call-done = f32[512,768]{1,0:T(8,128)} async-done(((f32[64,768]{1,0:T(8,128)}), f32[512,768]{1,0:T(8,128)}) %all-gather.10.cloned.1.call-update) | async-done | bytes 1572880 | tf_op jit(solution)/shard_map/all_gather | solution.py:41
  57.1 3.0 %fusion.8 = (f32[512]{0:T(512)S(1)}, f32[256]{0:T(256)S(1)}, f32[512,256]{1,0:T(8,128)S(1)}) fusion(f32[512,768]{1,0:T(8,128)} %all-gather.10.cloned.1.call-done, f32[256,768]{1,0:T(8,128)S(1)} %all_gather.30, f32[]{:T(128)} %bitcast.40), kind=kOutput, calls=%fused_computation.34 | convolution fusion | flops 1208352000 | bytes 2886660 | tf_op jit(solution)/shard_map/dot_general | solution.py:18
  60.1 0.2 exponential_reduce_fusion.1
  60.4 26.0 %all-gather.5 = f32[8,1,512]{2,1,0:T(1,128)S(1)} all-gather(f32[1,1,512]{2,1,0:T(1,128)S(1)} %bitcast.59), channel_id=3, replica_groups=mesh['blk'=8,'group'=4] {'blk'}, dimensions={0}, use_global_device_ids=true | all-gather | bytes 18432 | tf_op jit(solution)/shard_map/all_gather | solution.py:8
  86.4 26.0 %all-gather.4 = f32[8,1,512]{2,1,0:T(1,128)S(1)} all-gather(f32[1,1,512]{2,1,0:T(1,128)S(1)} %bitcast.57), channel_id=2, replica_groups=mesh['blk'=8,'group'=4] {'blk'}, dimensions={0}, use_global_device_ids=true | all-gather | bytes 18432 | tf_op jit(solution)/shard_map/all_gather | solution.py:8
  112.4 5.1 %all-gather.7 = f32[4,1,256]{2,1,0:T(1,128)S(1)} all-gather(f32[1,1,256]{2,1,0:T(1,128)S(1)} %bitcast.60), channel_id=5, replica_groups=mesh['blk'=8,'group'=4] {'group'}, dimensions={0}, use_global_device_ids=true | all-gather | bytes 5120 | tf_op jit(solution)/shard_map/all_gather | solution.py:8
  117.4 5.1 %all-gather.6 = f32[4,1,256]{2,1,0:T(1,128)S(1)} all-gather(f32[1,1,256]{2,1,0:T(1,128)S(1)} %bitcast.58), channel_id=4, replica_groups=mesh['blk'=8,'group'=4] {'group'}, dimensions={0}, use_global_device_ids=true | all-gather | bytes 5120 | tf_op jit(solution)/shard_map/all_gather | solution.py:8
  122.5 0.4 while.34
  122.9 0.2 while.35
  123.1 2.6 convolution_multiply_fusion.1
  125.7 0.0 reduce-scatter.5.cloned.1.call-update
  125.7 0.0 reduce-scatter.3.cloned.1.call-start
  125.8 2.7 %convolution_multiply_fusion = f32[512,768]{1,0:T(8,128)} fusion(f32[256,768]{1,0:T(8,128)S(1)} %all_gather.30, f32[]{:T(128)} %bitcast.39, f32[512,256]{1,0:T(8,128)S(1)} %get-tuple-element.311, f32[256]{0:T(256)S(1)} %log_add_fusion.1, f32[512]{0:T(512)S(1)} %log_add_fusion), kind=kOutput, calls=%fused_computation.6 | convolution fusion | flops 1208877056 | bytes 2886660 | tf_op jit(solution)/shard_map/dot_general | solution.py:80
  128.5 0.7 dynamic-slice_reduce_fusion
  130.5 0.9 multiply_reduce_fusion
  131.4 14.9 %reduce-scatter.5.cloned.1.call-done = f32[64,768]{1,0:T(8,128)} async-done(((f32[256,768]{1,0:T(8,128)}), f32[64,768]{1,0:T(8,128)}) %reduce-scatter.5.cloned.1.call-update) | async-done | bytes 196624 | tf_op jit(solution)/shard_map/reduce_scatter | solution.py:46
  146.4 68.7 %reduce-scatter.3.cloned.1.call-done = f32[64,768]{1,0:T(8,128)} async-done(((f32[512,768]{1,0:T(8,128)}), f32[64,768]{1,0:T(8,128)}) %reduce-scatter.3.cloned.1.call-update) | async-done | bytes 196624 | tf_op jit(solution)/shard_map/reduce_scatter | solution.py:43
  215.1 1.9 multiply_reduce_fusion.1
  217.0 0.6 multiply_reduce_fusion.2
  219.6 39.7 %all-reduce = (f32[]{:T(128)}, f32[]{:T(128)}) all-reduce(f32[]{:T(128)S(6)} %sub.94, f32[]{:T(128)S(6)} %sub.95), channel_id=1, replica_groups=mesh['blk'=8,'group'=4] {'blk','group'}, use_global_device_ids=true, to_apply=%region_14.0 | all-reduce | flops 2 | bytes 16 | tf_op jit(solution)/shard_map/psum | solution.py:100
  (38 shorter events, 0.4 us)
Async XLA Ops:
  7.2 49.9 %all-gather.10.cloned.1.call-start = ((), (), s32[]{:S(2)}) async-start(), calls=%async_computation.2 | async-start | bytes 1769472 | tf_op jit(solution)/shard_map/all_gather | solution.py:41
  7.9 138.5 %reduce-scatter.5.cloned.1.call-start = ((), (), s32[]{:S(2)}) async-start(), calls=%async_computation.4 | async-start | bytes 983040 | tf_op jit(solution)/shard_map/reduce_scatter | solution.py:46
  57.1 66.0 %copy-start = (f32[512,768]{1,0:T(8,128)S(1)}, f32[512,768]{1,0:T(8,128)}, u32[]{:S(2)}) copy-start(f32[512,768]{1,0:T(8,128)} %all-gather.10.cloned.1.call-done) | copy-start | bytes 4718596
  125.7 89.3 %reduce-scatter.3.cloned.1.call-start = ((), (), s32[]{:S(2)}) async-start(), calls=%async_computation.3 | async-start | bytes 1769472 | tf_op jit(solution)/shard_map/reduce_scatter | solution.py:43
  128.5 86.6 %copy-start.1 = (f32[64,768]{1,0:T(8,128)S(1)}, f32[64,768]{1,0:T(8,128)}, u32[]{:S(2)}) copy-start(f32[64,768]{1,0:T(8,128)} %param.7) | copy-start | bytes 589828
  128.5 86.6 %copy-start.2 = (f32[64,768]{1,0:T(8,128)S(1)}, f32[64,768]{1,0:T(8,128)}, u32[]{:S(2)}) copy-start(f32[64,768]{1,0:T(8,128)} %param.8) | copy-start | bytes 589828
Sparse Core Ops, SparseCore 0:
  10.2 46.8 all-gather.9
  125.8 20.4 reduce-scatter.4
  150.2 64.8 reduce-scatter.2
where the time goes:
time: 270 us; the launch traced here: 269 us
  waiting for transfers between devices  123 us (46%)
  blocking collectives  112 us (41%)
  between operations  21.3 us (8%)
  matrix products  8.33 us (3%)
  other arithmetic  4.61 us (2%)
    reduce_scatter x1, waiting for transfers between devices, body(): lax.psum_scatter(partial_sum, 'blk', scatter_dimension=0, tiled=True)  68.7 us
    all_gather x4, blocking collectives, combined_all(): everything = jax.tree.map(lambda part: lax.all_gather(part, axis), x)  62.1 us
    psum x1, blocking collectives, body(): lax.psum((loss_part, scale_part), ('blk', 'group'))  39.7 us
    all_gather x1, waiting for transfers between devices, body(): lax.all_gather(image_feats, 'blk', axis=0, tiled=True)  38.3 us
    reduce_scatter x1, waiting for transfers between devices, body(): lax.psum_scatter(partial_sum, 'group', scatter_dimension=0, tiled=True)  14.9 us
    all_gather x1, blocking collectives, body(): texts = lax.all_gather(text_feats, 'group', axis=0, tiled=True)  10.3 us
  transfers between devices with their start and end apart: 3, of which 3 were waited for; matrix products, arithmetic and copies ran while one was open for 2% of the time, Pallas kernels for 0%

commit v1 on v0

v1 whole, which is shorter than its diff:
```python
import functools

import jax
import jax.numpy as jnp
from jax import lax
from jax.experimental import pallas as pl
from jax.experimental.pallas import tpu as pltpu
from jax.sharding import PartitionSpec as P

F32 = jnp.float32
BF16 = jnp.bfloat16
MESH = pl.DeviceIdType.MESH
NT = (((1,), (1,)), ((), ()))
NN = (((1,), (0,)), ((), ()))


def dot(a, b, dims):
    return lax.dot_general(a, b, dims, preferred_element_type=F32)


def split2(x):
    hi = x.astype(BF16)
    return hi, (x - hi.astype(F32)).astype(BF16)


def split3(x):
    hi = x.astype(BF16)
    rest = x - hi.astype(F32)
    mid = rest.astype(BF16)
    return hi, mid, (rest - mid.astype(F32)).astype(BF16)


def tiles(count, fn):
    if count <= 2:
        for t in range(count):
            fn(t)
    else:
        lax.fori_loop(0, count, lambda t, c: (fn(t), c)[1], 0)


def span(t, step):
    start = t * step
    return pl.ds(start if isinstance(start, int) else pl.multiple_of(start, step), step)


def kernel(
    n_blk,
    n_group,
    width,
    scale_ref,
    image_ref,
    text_ref,
    image_grad_ref,
    text_grad_ref,
    loss_ref,
    scale_grad_ref,
    images,
    texts,
    scores,
    i_hi,
    i_mid,
    t_hi,
    t_mid,
    t_lo,
    w_hi,
    w_lo,
    wt_hi,
    wt_lo,
    part_i,
    part_t,
    from_core,
    from_y,
    from_g,
    from_x,
    from_f,
    row_stats,
    col_stats,
    totals_i,
    totals_t,
    send_sem,
    recv_sem,
):
    rows, emb = image_ref.shape
    chunks = emb // width
    n_g, n_x = n_blk // 4, n_group // 2
    half = n_blk // 2
    blk, group = lax.axis_index("blk"), lax.axis_index("group")
    f, r = blk // half, blk % half
    g, y = r // 2, r % 2
    x, core = group // 2, group % 2

    def device(f=f, g=g, y=y, x=x, core=core):
        return (f * half + g * 2 + y, x * 2 + core)

    def image_slot(g=g, y=y, core=core):
        return core * half + y * n_g + g

    def text_slot(x=x, f=f):
        return x * 2 + f

    image_peers = []
    for dc in range(2):
        for dy in range(2):
            for dg in range(n_g):
                if dc or dy or dg:
                    to = device(g=(g + dg) % n_g, y=(y + dy) % 2, core=(core + dc) % 2)
                    image_peers.append(((dg, dy, dc), ((n_g - dg) % n_g, dy, dc), to))
    text_peers = []
    for dx in range(n_x):
        for df in range(2):
            if dx or df:
                to = device(x=(x + dx) % n_x, f=(f + df) % 2)
                text_peers.append(((dx, df), ((n_x - dx) % n_x, df), to))

    barrier = pltpu.get_barrier_semaphore()
    for _, _, to in image_peers + text_peers:
        pl.semaphore_signal(barrier, inc=1, device_id=to, device_id_type=MESH)
    pl.semaphore_wait(barrier, len(image_peers) + len(text_peers))

    numbers = {}
    sent = []

    def number(name):
        return numbers.setdefault(name, len(numbers))

    def send(src, dst, to, out_name, in_name):
        copy = pltpu.make_async_remote_copy(
            src_ref=src,
            dst_ref=dst,
            send_sem=send_sem.at[number(("s",) + out_name)],
            recv_sem=recv_sem.at[number(("s",) + in_name)],
            device_id=to,
            device_id_type=MESH,
        )
        copy.start()
        sent.append(copy)

    def arrived(dst, name):
        pltpu.make_async_remote_copy(
            src_ref=dst,
            dst_ref=dst,
            send_sem=send_sem.at[number(("s",) + name)],
            recv_sem=recv_sem.at[number(("s",) + name)],
            device_id=device(core=1 - core),
            device_id_type=MESH,
        ).wait_recv()

    def cols(k):
        return pl.ds(k * width, width)

    def block(ref, slot, k, count=1):
        return ref.at[pl.ds(pl.multiple_of(slot * rows, rows), count * rows), cols(k)]

    own_i, own_t = image_slot(), text_slot()
    y2, f2, core2 = 1 - y, 1 - f, 1 - core

    for k in range(chunks):
        mine_i, mine_t = image_ref.at[:, cols(k)], text_ref.at[:, cols(k)]
        for dg in range(1, n_g):
            send(mine_i, block(images, own_i, k), device(g=(g + dg) % n_g), ("ig", dg, k), ("ig", n_g - dg, k))
        send(mine_t, block(texts, own_t, k), device(f=f2), ("tf", k), ("tf", k))
        send(mine_i, block(images, own_i, k), device(y=y2), ("iy", 0, k), ("iy", 0, k))
        for dx in range(1, n_x):
            send(mine_t, block(texts, own_t, k), device(x=(x + dx) % n_x), ("tx", dx, 0, k), ("tx", n_x - dx, 0, k))
        send(mine_i, block(images, own_i, k), device(core=core2), ("ic", 0, 0, k), ("ic", 0, 0, k))
    images[pl.ds(pl.multiple_of(own_i * rows, rows), rows), :] = image_ref[...]
    texts[pl.ds(pl.multiple_of(own_t * rows, rows), rows), :] = text_ref[...]

    def relay(k):
        for dg in range(1, n_g):
            at = block(images, image_slot(g=(g + dg) % n_g), k)
            arrived(at, ("ig", dg, k))
            send(at, at, device(y=y2), ("iy", dg, k), ("iy", dg, k))
            send(at, at, device(core=core2), ("ic", dg, 0, k), ("ic", dg, 0, k))
        at = block(texts, text_slot(f=f2), k)
        arrived(at, ("tf", k))
        for dx in range(1, n_x):
            send(at, at, device(x=(x + dx) % n_x), ("tx", dx, 1, k), ("tx", n_x - dx, 1, k))
        at = block(images, image_slot(y=y2), k)
        arrived(at, ("iy", 0, k))
        send(at, at, device(core=core2), ("ic", 0, 1, k), ("ic", 0, 1, k))

    def relay_last(k):
        for dg in range(1, n_g):
            at = block(images, image_slot(g=(g + dg) % n_g, y=y2), k)
            arrived(at, ("iy", dg, k))
            send(at, at, device(core=core2), ("ic", dg, 1, k), ("ic", dg, 1, k))

    def collect(k):
        for dx in range(1, n_x):
            for df in range(2):
                arrived(block(texts, text_slot(x=(x + dx) % n_x, f=(f + df) % 2), k), ("tx", dx, df, k))
        for dg in range(n_g):
            for dy in range(2):
                at = block(images, image_slot(g=(g + dg) % n_g, y=(y + dy) % 2, core=core2), k)
                arrived(at, ("ic", dg, dy, k))

    scale = scale_ref[0]
    n_images, n_texts = images.shape[0], texts.shape[0]
    step = min(256, n_images)
    steps = n_images // step

    def score(k):
        col = cols(k)
        hi, mid, lo = split3(texts[:, col])
        t_hi[:, col], t_mid[:, col], t_lo[...] = hi, mid, lo

        def tile(t):
            part = span(t, step)
            a_hi, a_mid, a_lo = split3(images[part, col])
            i_hi[part, col], i_mid[part, col] = a_hi, a_mid
            b_hi, b_mid, b_lo = t_hi[:, col], t_mid[:, col], t_lo[...]
            total = dot(a_lo, b_hi, NT) + dot(a_hi, b_lo, NT) + dot(a_mid, b_mid, NT)
            total = total + dot(a_mid, b_hi, NT) + dot(a_hi, b_mid, NT)
            total = total + dot(a_hi, b_hi, NT)
            if k > 0:
                total = total + scores[part, :]
            if k == chunks - 1:
                total = scale * total
            scores[part, :] = total

        tiles(steps, tile)

    relay(0)
    for k in range(chunks):
        relay_last(k)
        if k + 1 < chunks:
            relay(k + 1)
        collect(k)
        score(k)

    def to_lanes(column):
        return jnp.transpose(jnp.broadcast_to(column, (column.shape[0], 128)))[0:1, :]

    def to_rows(line):
        return jnp.transpose(jnp.broadcast_to(line, (128, line.shape[1])))[:, 0:1]

    col_stats[own_t] = jnp.full((1, n_texts), -3e38, F32)

    def row_tile(t):
        part = span(t, step)
        s = scores[part, :]
        top = jnp.max(s, axis=1, keepdims=True)
        total = jnp.sum(jnp.exp(s - top), axis=1, keepdims=True)
        row_stats[own_i, :, part] = to_lanes(top + jnp.log(total))
        col_stats[own_t] = jnp.maximum(col_stats[own_t], jnp.max(s, axis=0, keepdims=True))

    tiles(steps, row_tile)
    for (dg, dy, dc), back, to in image_peers:
        here = row_stats.at[own_i]
        send(here, here, to, ("rs", dg, dy, dc), ("rs",) + back)

    col_top = col_stats[own_t]
    col_stats[own_t] = jnp.zeros((1, n_texts), F32)

    def col_tile(t):
        s = scores[span(t, step), :]
        col_stats[own_t] = col_stats[own_t] + jnp.sum(jnp.exp(s - col_top), axis=0, keepdims=True)

    tiles(steps, col_tile)
    col_stats[own_t] = col_top + jnp.log(col_stats[own_t])
    for (dx, df), back, to in text_peers:
        here = col_stats.at[own_t]
        send(here, here, to, ("cs", dx, df), ("cs",) + back)

    diagonal = scale * jnp.sum(image_ref[...] * text_ref[...])

    for (dg, dy, dc), _, _ in image_peers:
        slot = image_slot((g + dg) % n_g, (y + dy) % 2, (core + dc) % 2)
        arrived(row_stats.at[slot], ("rs", dg, dy, dc))
    for (dx, df), _, _ in text_peers:
        arrived(col_stats.at[text_slot((x + dx) % n_x, (f + df) % 2)], ("cs", dx, df))

    def merged(stats):
        every = stats[...]
        top = jnp.max(every, axis=0)
        return top + jnp.log(jnp.sum(jnp.exp(every - top[None]), axis=0))

    row_lse, col_lse = merged(row_stats), merged(col_stats)

    weighted = jnp.zeros((1, n_texts), F32)
    for t in range(steps):
        part = span(t, step)
        s = scores[part, :]
        w = 0.5 * (jnp.exp(s - to_rows(row_lse[:, t * step : (t + 1) * step])) + jnp.exp(s - col_lse))
        weighted = weighted + jnp.sum(w * s, axis=0, keepdims=True)
        w_hi[part, :], w_lo[part, :] = split2(w)
        wt_hi[:, part], wt_lo[:, part] = split2(jnp.transpose(w))

    t_step = min(256, n_texts)

    def partial_texts(k):
        col = cols(k)

        def tile(t):
            part = span(t, t_step)
            a_hi, a_lo, b_hi, b_lo = wt_hi[part, :], wt_lo[part, :], i_hi[:, col], i_mid[:, col]
            part_t[part, col] = dot(a_lo, b_hi, NN) + dot(a_hi, b_lo, NN) + dot(a_hi, b_hi, NN)

        tiles(n_texts // t_step, tile)

    def partial_images(k):
        col = cols(k)

        def tile(t):
            part = span(t, step)
            a_hi, a_lo, b_hi, b_lo = w_hi[part, :], w_lo[part, :], t_hi[:, col], t_mid[:, col]
            part_i[part, col] = dot(a_lo, b_hi, NN) + dot(a_hi, b_lo, NN) + dot(a_hi, b_hi, NN)

        tiles(steps, tile)

    for k in range(chunks):
        partial_images(k)
        send(block(part_i, core2 * half, k, half), from_core.at[:, cols(k)], device(core=core2), ("bc", k), ("bc", k))
        partial_texts(k)
        for dx in range(1, n_x):
            xx = (x + dx) % n_x
            src, dst = block(part_t, xx * 2, k, 2), from_x.at[n_x - dx - 1, :, cols(k)]
            send(src, dst, device(x=xx), ("bx", dx, k), ("bx", n_x - dx, k))

    row_lane = lax.broadcasted_iota(jnp.int32, (1, n_images), 1) // rows
    col_lane = lax.broadcasted_iota(jnp.int32, (1, n_texts), 1) // rows
    own_rows = jnp.sum(jnp.where(row_lane == own_i, row_lse, 0.0))
    own_cols = jnp.sum(jnp.where(col_lane == own_t, col_lse, 0.0))
    loss_part = 0.5 * own_rows + 0.5 * own_cols - diagonal
    scale_part = jnp.sum(weighted) - diagonal
    lane = lax.broadcasted_iota(jnp.int32, (1, 128), 1)
    totals_i[own_i] = jnp.where(lane == 0, loss_part, jnp.where(lane == 1, scale_part, 0.0))
    for (dg, dy, dc), back, to in image_peers:
        here = totals_i.at[own_i]
        send(here, here, to, ("ti", dg, dy, dc), ("ti",) + back)

    def rows_of(slot, count=1):
        return pl.ds(pl.multiple_of(slot * rows, rows), count * rows)

    base = core * half
    for k in range(chunks):
        col = cols(k)
        arrived(from_core.at[:, col], ("bc", k))
        away = rows_of(base + y2 * n_g, n_g)
        part_i[away, col] = part_i[away, col] + from_core[rows_of(y2 * n_g, n_g), col]
        send(part_i.at[away, col], from_y.at[:, col], device(y=y2), ("by", k), ("by", k))
        keep = rows_of(base + y * n_g, n_g)
        part_i[keep, col] = part_i[keep, col] + from_core[rows_of(y * n_g, n_g), col]

    for k in range(chunks):
        col = cols(k)
        for dx in range(1, n_x):
            arrived(from_x.at[dx - 1, :, col], ("bx", dx, k))
        away, keep = rows_of(x * 2 + f2), rows_of(x * 2 + f)
        total_away, total_keep = part_t[away, col], part_t[keep, col]
        for dx in range(1, n_x):
            total_away = total_away + from_x[dx - 1, rows_of(f2), col]
            total_keep = total_keep + from_x[dx - 1, rows_of(f), col]
        part_t[away, col] = total_away
        send(part_t.at[away, col], from_f.at[:, col], device(f=f2), ("bf", k), ("bf", k))
        part_t[keep, col] = total_keep

        arrived(from_y.at[:, col], ("by", k))
        for dg in range(1, n_g):
            gg = (g + dg) % n_g
            away = rows_of(base + y * n_g + gg)
            part_i[away, col] = part_i[away, col] + from_y[rows_of(gg), col]
            dst = from_g.at[n_g - dg - 1, :, col]
            send(part_i.at[away, col], dst, device(g=gg), ("bg", dg, k), ("bg", n_g - dg, k))

    for (dg, dy, dc), _, _ in image_peers:
        slot = image_slot((g + dg) % n_g, (y + dy) % 2, (core + dc) % 2)
        arrived(totals_i.at[slot], ("ti", dg, dy, dc))
    totals_t[own_t] = jnp.sum(totals_i[...], axis=0)
    for (dx, df), back, to in text_peers:
        here = totals_t.at[own_t]
        send(here, here, to, ("tt", dx, df), ("tt",) + back)

    for k in range(chunks):
        col = cols(k)
        arrived(from_f.at[:, col], ("bf", k))
        total = part_t[rows_of(x * 2 + f), col] + from_f[:, col]
        text_grad_ref[:, col] = scale * (total - image_ref[:, col])
        total = part_i[rows_of(own_i), col] + from_y[rows_of(g), col]
        for dg in range(1, n_g):
            arrived(from_g.at[dg - 1, :, col], ("bg", dg, k))
            total = total + from_g[dg - 1, :, col]
        image_grad_ref[:, col] = scale * (total - text_ref[:, col])

    for (dx, df), _, _ in text_peers:
        arrived(totals_t.at[text_slot((x + dx) % n_x, (f + df) % 2)], ("tt", dx, df))
    total = jnp.sum(totals_t[...], axis=0)
    batch = rows * n_blk * n_group
    loss_ref[0] = jnp.sum(jnp.where(lane == 0, total, 0.0)) / batch
    scale_grad_ref[0] = jnp.sum(jnp.where(lane == 1, total, 0.0)) / (scale * batch)

    for copy in sent:
        copy.wait_send()


def body(n_blk, n_group, image_feats, text_feats, logit_scale):
    rows, emb = image_feats.shape
    width = 256 if emb % 256 == 0 else emb
    chunks = emb // width
    n_g, n_x = n_blk // 4, n_group // 2
    n_images, n_texts = rows * n_blk, rows * n_group
    count = chunks * (n_g * 4 + n_x * 4 + 8) + 2 * (n_blk + n_group)
    vmem = pl.BlockSpec(memory_space=pltpu.VMEM)
    smem = pl.BlockSpec(memory_space=pltpu.SMEM)
    image_grad, text_grad, mean_loss, scale_grad = pl.pallas_call(
        functools.partial(kernel, n_blk, n_group, width),
        out_shape=(
            jax.ShapeDtypeStruct((rows, emb), F32),
            jax.ShapeDtypeStruct((rows, emb), F32),
            jax.ShapeDtypeStruct((1,), F32),
            jax.ShapeDtypeStruct((1,), F32),
        ),
        in_specs=[smem, vmem, vmem],
        out_specs=(vmem, vmem, smem, smem),
        scratch_shapes=[
            pltpu.VMEM((n_images, emb), F32),
            pltpu.VMEM((n_texts, emb), F32),
            pltpu.VMEM((n_images, n_texts), F32),
            pltpu.VMEM((n_images, emb), BF16),
            pltpu.VMEM((n_images, emb), BF16),
            pltpu.VMEM((n_texts, emb), BF16),
            pltpu.VMEM((n_texts, emb), BF16),
            pltpu.VMEM((n_texts, width), BF16),
            pltpu.VMEM((n_images, n_texts), BF16),
            pltpu.VMEM((n_images, n_texts), BF16),
            pltpu.VMEM((n_texts, n_images), BF16),
            pltpu.VMEM((n_texts, n_images), BF16),
            pltpu.VMEM((n_images, emb), F32),
            pltpu.VMEM((n_texts, emb), F32),
            pltpu.VMEM((n_images // 2, emb), F32),
            pltpu.VMEM((n_g * rows, emb), F32),
            pltpu.VMEM((max(n_g - 1, 1), rows, emb), F32),
            pltpu.VMEM((max(n_x - 1, 1), 2 * rows, emb), F32),
            pltpu.VMEM((rows, emb), F32),
            pltpu.VMEM((n_blk, 1, n_images), F32),
            pltpu.VMEM((n_group, 1, n_texts), F32),
            pltpu.VMEM((n_blk, 1, 128), F32),
            pltpu.VMEM((n_group, 1, 128), F32),
            pltpu.SemaphoreType.DMA((count,)),
            pltpu.SemaphoreType.DMA((count,)),
        ],
        compiler_params=pltpu.CompilerParams(
            collective_id=0, has_side_effects=True, vmem_limit_bytes=56 * 1024 * 1024
        ),
        name="contrastive",
    )(logit_scale, image_feats, text_feats)
    return image_grad, text_grad, mean_loss, scale_grad


def solution(mesh):
    return jax.shard_map(
        functools.partial(body, mesh.shape["blk"], mesh.shape["group"]),
        mesh=mesh,
        in_specs=(P(("blk", "group"), None), P(("blk", "group"), None), P()),
        out_specs=(P(("blk", "group"), None), P(("blk", "group"), None), P(), P()),
        check_vma=False,
    )
```

time: 270 us -> 53.9 us (0.20)
  waiting for transfers between devices: 123 us -> 0 us
  blocking collectives: 112 us -> 0 us
  Pallas kernels: 0 us -> 46.6 us
  between operations: 21.3 us -> 4.81 us
  matrix products: 8.33 us -> 0 us
  other arithmetic: 4.61 us -> 0 us
    reduce_scatter x2 -> x0, waiting for transfers between devices: 83.6 us -> none  [the longest x1 68.7 us: body(): lax.psum_scatter(partial_sum, 'blk', scatter_dimension=0, tiled=True)]
    all_gather x5 -> x0, blocking collectives: 72.4 us -> none  [the longest x4 62.1 us: combined_all(): everything = jax.tree.map(lambda part: lax.all_gather(part, axis), x)]
    pallas_call x0 -> x1, Pallas kernels: none -> 46.6 us  [body(): pl.pallas_call(functools.partial(kernel, n_blk, n_group, width), out_shap...]
    psum x1 -> x0, blocking collectives: 39.7 us -> none  [body(): lax.psum((loss_part, scale_part), ('blk', 'group'))]
    all_gather x1 -> x0, waiting for transfers between devices: 38.3 us -> none  [body(): lax.all_gather(image_feats, 'blk', axis=0, tiled=True)]
    dot_general x3 -> x0, matrix products: 8.33 us -> none  [the longest x1 3.03 us: scores_of(): lax.dot_general(pieces, texts, (((1,), (1,)), ((), ())), precision=lax.Pr...]
    reduce_sum x5 -> x0, other arithmetic: 4.38 us -> none  [the longest x1 1.91 us: body(): diagonal = scale * jnp.sum(image_feats * text_feats, axis=1)]
  transfers between devices with their start and end apart: 3 -> 0, of which waited for: 3 -> 0; matrix products, arithmetic and copies ran while one was open for 2% -> 0% of each run, Pallas kernels for 0% -> 0%
where the time goes in v1:
time: 53.9 us; the launch traced here: 53.7 us
  Pallas kernels  46.6 us (86%)
  between operations  4.81 us (9%)
  local copies, waits for them, and re-layouts  2.34 us (4%)
    pallas_call x1, Pallas kernels, body(): pl.pallas_call(functools.partial(kernel, n_blk, n_group, width), out_shap...  46.6 us
    unnamed x4, local copies, waits for them, and re-layouts  2.34 us

profile of v1, /device:TPU:0, one launch (start us, length us, event | category | flops | bytes accessed | tf_op | source)
XLA Modules:
  0.0 53.7 jit_solution(6416202838485679333)
XLA Ops:
  1.3 46.6 %contrastive.1 = (f32[64,768]{1,0:T(8,128)}, f32[64,768]{1,0:T(8,128)}, f32[1]{0:T(128)}, f32[1]{0:T(128)}) custom-call(f32[1]{0:T(128)S(6)} %copy.11.scale_ref, f32[64,768]{1,0:T(8,128)} %image_ref.1, f32[64,768]{1,0:T(8,128)} %text_ref.1), custom_call_target="tpu_custom_call" | custom-call | tf_op jit(solution)/shard_map/contrastive/pallas_call | solution.py:406
  47.9 0.0 copy-start
  47.9 1.7 %copy.12 = f32[64,768]{1,0:T(8,128)} copy(f32[64,768]{1,0:T(8,128)} %get-tuple-element.8) | data formatting | bytes 393216
  49.5 0.0 copy-done
  49.5 0.7 %copy.13 = f32[64,768]{1,0:T(8,128)} copy(f32[64,768]{1,0:T(8,128)S(1)} %copy-done) | data formatting | bytes 393216
Async XLA Ops:
  47.9 1.7 %copy-start = (f32[64,768]{1,0:T(8,128)S(1)}, f32[64,768]{1,0:T(8,128)}, u32[]{:S(2)}) copy-start(f32[64,768]{1,0:T(8,128)} %get-tuple-element.9) | copy-start | bytes 589828

commit v2 on v1

--- a/solution.py
+++ b/solution.py
@@ -12,6 +12,11 @@
 MESH = pl.DeviceIdType.MESH
 NT = (((1,), (1,)), ((), ()))
 NN = (((1,), (0,)), ((), ()))
+
+
+LINK_WIDTH = 256
+AHEAD = 2
+BACK_AHEAD = 2
 
 
 def dot(a, b, dims):
@@ -82,6 +87,8 @@
 ):
     rows, emb = image_ref.shape
     chunks = emb // width
+    link = LINK_WIDTH if width % LINK_WIDTH == 0 else width
+    links, ratio = emb // link, width // link
     n_g, n_x = n_blk // 4, n_group // 2
     half = n_blk // 2
     blk, group = lax.axis_index("blk"), lax.axis_index("group")
@@ -148,21 +155,28 @@
     def cols(k):
         return pl.ds(k * width, width)
 
+    def lcols(k):
+        return pl.ds(k * link, link)
+
     def block(ref, slot, k, count=1):
-        return ref.at[pl.ds(pl.multiple_of(slot * rows, rows), count * rows), cols(k)]
+        return ref.at[pl.ds(pl.multiple_of(slot * rows, rows), count * rows), lcols(k)]
 
     own_i, own_t = image_slot(), text_slot()
     y2, f2, core2 = 1 - y, 1 - f, 1 - core
 
-    for k in range(chunks):
-        mine_i, mine_t = image_ref.at[:, cols(k)], text_ref.at[:, cols(k)]
+    def begin(k):
+        mine_i, mine_t = image_ref.at[:, lcols(k)], text_ref.at[:, lcols(k)]
+        send(mine_t, block(texts, own_t, k), device(f=f2), ("tf", k), ("tf", k))
         for dg in range(1, n_g):
             send(mine_i, block(images, own_i, k), device(g=(g + dg) % n_g), ("ig", dg, k), ("ig", n_g - dg, k))
-        send(mine_t, block(texts, own_t, k), device(f=f2), ("tf", k), ("tf", k))
         send(mine_i, block(images, own_i, k), device(y=y2), ("iy", 0, k), ("iy", 0, k))
         for dx in range(1, n_x):
             send(mine_t, block(texts, own_t, k), device(x=(x + dx) % n_x), ("tx", dx, 0, k), ("tx", n_x - dx, 0, k))
         send(mine_i, block(images, own_i, k), device(core=core2), ("ic", 0, 0, k), ("ic", 0, 0, k))
+
+    ahead = min(AHEAD, links)
+    for k in range(ahead):
+        begin(k)
     images[pl.ds(pl.multiple_of(own_i * rows, rows), rows), :] = image_ref[...]
     texts[pl.ds(pl.multiple_of(own_t * rows, rows), rows), :] = text_ref[...]
 
@@ -221,13 +235,17 @@
 
         tiles(steps, tile)
 
-    relay(0)
-    for k in range(chunks):
-        relay_last(k)
-        if k + 1 < chunks:
-            relay(k + 1)
-        collect(k)
-        score(k)
+    for k in range(links + 2):
+        if k < links:
+            relay(k)
+        if k + ahead < links:
+            begin(k + ahead)
+        if 1 <= k <= links:
+            relay_last(k - 1)
+        if k >= 2:
+            collect(k - 2)
+            if (k - 1) % ratio == 0:
+                score((k - 1) // ratio - 1)
 
     def to_lanes(column):
         return jnp.transpose(jnp.broadcast_to(column, (column.shape[0], 128)))[0:1, :]
@@ -309,14 +327,66 @@
 
         tiles(steps, tile)
 
+    def rows_of(slot, count=1):
+        return pl.ds(pl.multiple_of(slot * rows, rows), count * rows)
+
+    def send_x(k):
+        for dx in range(1, n_x):
+            xx = (x + dx) % n_x
+            src, dst = block(part_t, xx * 2, k, 2), from_x.at[n_x - dx - 1, :, lcols(k)]
+            send(src, dst, device(x=xx), ("bx", dx, k), ("bx", n_x - dx, k))
+
+    def send_core(k):
+        src, dst = block(part_i, core2 * half, k, half), from_core.at[:, lcols(k)]
+        send(src, dst, device(core=core2), ("bc", k), ("bc", k))
+
+    base = core * half
+
+    def send_y(k):
+        col = lcols(k)
+        arrived(from_core.at[:, col], ("bc", k))
+        away = rows_of(base + y2 * n_g, n_g)
+        part_i[away, col] = part_i[away, col] + from_core[rows_of(y2 * n_g, n_g), col]
+        send(part_i.at[away, col], from_y.at[:, col], device(y=y2), ("by", k), ("by", k))
+        keep = rows_of(base + y * n_g, n_g)
+        part_i[keep, col] = part_i[keep, col] + from_core[rows_of(y * n_g, n_g), col]
+
+    def send_f(k):
+        col = lcols(k)
+        for dx in range(1, n_x):
+            arrived(from_x.at[dx - 1, :, col], ("bx", dx, k))
+        away, keep = rows_of(x * 2 + f2), rows_of(x * 2 + f)
+        total = part_t[away, col]
+        for dx in range(1, n_x):
+            total = total + from_x[dx - 1, rows_of(f2), col]
+        part_t[away, col] = total
+        send(part_t.at[away, col], from_f.at[:, col], device(f=f2), ("bf", k), ("bf", k))
+        total = part_t[keep, col]
+        for dx in range(1, n_x):
+            total = total + from_x[dx - 1, rows_of(f), col]
+        part_t[keep, col] = total
+
+    def send_g(k):
+        col = lcols(k)
+        arrived(from_y.at[:, col], ("by", k))
+        for dg in range(1, n_g):
+            gg = (g + dg) % n_g
+            away = rows_of(base + y * n_g + gg)
+            part_i[away, col] = part_i[away, col] + from_y[rows_of(gg), col]
+            dst = from_g.at[n_g - dg - 1, :, col]
+            send(part_i.at[away, col], dst, device(g=gg), ("bg", dg, k), ("bg", n_g - dg, k))
+
+    behind = min(BACK_AHEAD, links)
     for k in range(chunks):
+        partial_texts(k)
+        for j in range(k * ratio, (k + 1) * ratio):
+            if j < behind:
+                send_x(j)
         partial_images(k)
-        send(block(part_i, core2 * half, k, half), from_core.at[:, cols(k)], device(core=core2), ("bc", k), ("bc", k))
-        partial_texts(k)
-        for dx in range(1, n_x):
-            xx = (x + dx) % n_x
-            src, dst = block(part_t, xx * 2, k, 2), from_x.at[n_x - dx - 1, :, cols(k)]
-            send(src, dst, device(x=xx), ("bx", dx, k), ("bx", n_x - dx, k))
+        for j in range(k * ratio, (k + 1) * ratio):
+            send_core(j)
+            if j < behind:
+                send_y(j)
 
     row_lane = lax.broadcasted_iota(jnp.int32, (1, n_images), 1) // rows
     col_lane = lax.broadcasted_iota(jnp.int32, (1, n_texts), 1) // rows
@@ -330,39 +400,13 @@
         here = totals_i.at[own_i]
         send(here, here, to, ("ti", dg, dy, dc), ("ti",) + back)
 
-    def rows_of(slot, count=1):
-        return pl.ds(pl.multiple_of(slot * rows, rows), count * rows)
-
-    base = core * half
-    for k in range(chunks):
-        col = cols(k)
-        arrived(from_core.at[:, col], ("bc", k))
-        away = rows_of(base + y2 * n_g, n_g)
-        part_i[away, col] = part_i[away, col] + from_core[rows_of(y2 * n_g, n_g), col]
-        send(part_i.at[away, col], from_y.at[:, col], device(y=y2), ("by", k), ("by", k))
-        keep = rows_of(base + y * n_g, n_g)
-        part_i[keep, col] = part_i[keep, col] + from_core[rows_of(y * n_g, n_g), col]
-
-    for k in range(chunks):
-        col = cols(k)
-        for dx in range(1, n_x):
-            arrived(from_x.at[dx - 1, :, col], ("bx", dx, k))
-        away, keep = rows_of(x * 2 + f2), rows_of(x * 2 + f)
-        total_away, total_keep = part_t[away, col], part_t[keep, col]
-        for dx in range(1, n_x):
-            total_away = total_away + from_x[dx - 1, rows_of(f2), col]
-            total_keep = total_keep + from_x[dx - 1, rows_of(f), col]
-        part_t[away, col] = total_away
-        send(part_t.at[away, col], from_f.at[:, col], device(f=f2), ("bf", k), ("bf", k))
-        part_t[keep, col] = total_keep
-
-        arrived(from_y.at[:, col], ("by", k))
-        for dg in range(1, n_g):
-            gg = (g + dg) % n_g
-            away = rows_of(base + y * n_g + gg)
-            part_i[away, col] = part_i[away, col] + from_y[rows_of(gg), col]
-            dst = from_g.at[n_g - dg - 1, :, col]
-            send(part_i.at[away, col], dst, device(g=gg), ("bg", dg, k), ("bg", n_g - dg, k))
+    for k in range(links):
+        send_f(k)
+        if k + behind < links:
+            send_x(k + behind)
+        send_g(k)
+        if k + behind < links:
+            send_y(k + behind)
 
     for (dg, dy, dc), _, _ in image_peers:
         slot = image_slot((g + dg) % n_g, (y + dy) % 2, (core + dc) % 2)
@@ -372,8 +416,8 @@
         here = totals_t.at[own_t]
         send(here, here, to, ("tt", dx, df), ("tt",) + back)
 
-    for k in range(chunks):
-        col = cols(k)
+    for k in range(links):
+        col = lcols(k)
         arrived(from_f.at[:, col], ("bf", k))
         total = part_t[rows_of(x * 2 + f), col] + from_f[:, col]
         text_grad_ref[:, col] = scale * (total - image_ref[:, col])
@@ -397,10 +441,10 @@
 def body(n_blk, n_group, image_feats, text_feats, logit_scale):
     rows, emb = image_feats.shape
     width = 256 if emb % 256 == 0 else emb
-    chunks = emb // width
     n_g, n_x = n_blk // 4, n_group // 2
     n_images, n_texts = rows * n_blk, rows * n_group
-    count = chunks * (n_g * 4 + n_x * 4 + 8) + 2 * (n_blk + n_group)
+    links = emb // (LINK_WIDTH if width % LINK_WIDTH == 0 else width)
+    count = links * (n_g * 4 + n_x * 4 + 8) + 2 * (n_blk + n_group)
     vmem = pl.BlockSpec(memory_space=pltpu.VMEM)
     smem = pl.BlockSpec(memory_space=pltpu.SMEM)
     image_grad, text_grad, mean_loss, scale_grad = pl.pallas_call(

time: 53.9 us -> 52 us (0.965)
  Pallas kernels: 46.6 us -> 44.6 us
    pallas_call x1, Pallas kernels: 46.6 us -> 44.6 us  [body(): pl.pallas_call(functools.partial(kernel, n_blk, n_group, width), out_shap...]
where the time goes in v2:
time: 52 us; the launch traced here: 51.8 us
  Pallas kernels  44.6 us (86%)
  between operations  4.81 us (9%)
  local copies, waits for them, and re-layouts  2.34 us (4%)
    pallas_call x1, Pallas kernels, body(): pl.pallas_call(functools.partial(kernel, n_blk, n_group, width), out_shap...  44.6 us
    unnamed x4, local copies, waits for them, and re-layouts  2.34 us

profile of v2, /device:TPU:0, one launch (start us, length us, event | category | flops | bytes accessed | tf_op | source)
XLA Modules:
  0.0 51.8 jit_solution(1100684082960270117)
XLA Ops:
  1.3 44.6 %contrastive.1 = (f32[64,768]{1,0:T(8,128)}, f32[64,768]{1,0:T(8,128)}, f32[1]{0:T(128)}, f32[1]{0:T(128)}) custom-call(f32[1]{0:T(128)S(6)} %copy.11.scale_ref, f32[64,768]{1,0:T(8,128)} %image_ref.1, f32[64,768]{1,0:T(8,128)} %text_ref.1), custom_call_target="tpu_custom_call" | custom-call | tf_op jit(solution)/shard_map/contrastive/pallas_call | solution.py:450
  45.9 0.0 copy-start
  45.9 1.7 %copy.12 = f32[64,768]{1,0:T(8,128)} copy(f32[64,768]{1,0:T(8,128)} %get-tuple-element.8) | data formatting | bytes 393216
  47.6 0.0 copy-done
  47.6 0.7 %copy.13 = f32[64,768]{1,0:T(8,128)} copy(f32[64,768]{1,0:T(8,128)S(1)} %copy-done) | data formatting | bytes 393216
Async XLA Ops:
  45.9 1.7 %copy-start = (f32[64,768]{1,0:T(8,128)S(1)}, f32[64,768]{1,0:T(8,128)}, u32[]{:S(2)}) copy-start(f32[64,768]{1,0:T(8,128)} %get-tuple-element.9) | copy-start | bytes 589828

commit v3 on v2

--- a/solution.py
+++ b/solution.py
@@ -16,7 +16,7 @@
 
 LINK_WIDTH = 256
 AHEAD = 2
-BACK_AHEAD = 2
+EARLY = 1
 
 
 def dot(a, b, dims):
@@ -84,6 +84,7 @@
     totals_t,
     send_sem,
     recv_sem,
+    load_sem,
 ):
     rows, emb = image_ref.shape
     chunks = emb // width
@@ -119,10 +120,21 @@
                 to = device(x=(x + dx) % n_x, f=(f + df) % 2)
                 text_peers.append(((dx, df), ((n_x - dx) % n_x, df), to))
 
+    own_i, own_t = image_slot(), text_slot()
+    own_images = pl.ds(pl.multiple_of(own_i * rows, rows), rows)
+    own_texts = pl.ds(pl.multiple_of(own_t * rows, rows), rows)
+    loads = [
+        pltpu.make_async_copy(image_ref, images.at[own_images], load_sem.at[0]),
+        pltpu.make_async_copy(text_ref, texts.at[own_texts], load_sem.at[1]),
+    ]
     barrier = pltpu.get_barrier_semaphore()
-    for _, _, to in image_peers + text_peers:
+    for _, _, to in text_peers + image_peers:
         pl.semaphore_signal(barrier, inc=1, device_id=to, device_id_type=MESH)
+    for load in loads:
+        load.start()
     pl.semaphore_wait(barrier, len(image_peers) + len(text_peers))
+    for load in loads:
+        load.wait()
 
     numbers = {}
     sent = []
@@ -161,11 +173,10 @@
     def block(ref, slot, k, count=1):
         return ref.at[pl.ds(pl.multiple_of(slot * rows, rows), count * rows), lcols(k)]
 
-    own_i, own_t = image_slot(), text_slot()
     y2, f2, core2 = 1 - y, 1 - f, 1 - core
 
     def begin(k):
-        mine_i, mine_t = image_ref.at[:, lcols(k)], text_ref.at[:, lcols(k)]
+        mine_i, mine_t = block(images, own_i, k), block(texts, own_t, k)
         send(mine_t, block(texts, own_t, k), device(f=f2), ("tf", k), ("tf", k))
         for dg in range(1, n_g):
             send(mine_i, block(images, own_i, k), device(g=(g + dg) % n_g), ("ig", dg, k), ("ig", n_g - dg, k))
@@ -177,8 +188,6 @@
     ahead = min(AHEAD, links)
     for k in range(ahead):
         begin(k)
-    images[pl.ds(pl.multiple_of(own_i * rows, rows), rows), :] = image_ref[...]
-    texts[pl.ds(pl.multiple_of(own_t * rows, rows), rows), :] = text_ref[...]
 
     def relay(k):
         for dg in range(1, n_g):
@@ -281,7 +290,7 @@
         here = col_stats.at[own_t]
         send(here, here, to, ("cs", dx, df), ("cs",) + back)
 
-    diagonal = scale * jnp.sum(image_ref[...] * text_ref[...])
+    diagonal = scale * jnp.sum(images[own_images, :] * texts[own_texts, :])
 
     for (dg, dy, dc), _, _ in image_peers:
         slot = image_slot((g + dg) % n_g, (y + dy) % 2, (core + dc) % 2)
@@ -360,7 +369,7 @@
         for dx in range(1, n_x):
             total = total + from_x[dx - 1, rows_of(f2), col]
         part_t[away, col] = total
-        send(part_t.at[away, col], from_f.at[:, col], device(f=f2), ("bf", k), ("bf", k))
+        send(part_t.at[away, col], from_f.at[x, :, col], device(f=f2), ("bf", 0, k), ("bf", 0, k))
         total = part_t[keep, col]
         for dx in range(1, n_x):
             total = total + from_x[dx - 1, rows_of(f), col]
@@ -373,20 +382,72 @@
             gg = (g + dg) % n_g
             away = rows_of(base + y * n_g + gg)
             part_i[away, col] = part_i[away, col] + from_y[rows_of(gg), col]
-            dst = from_g.at[n_g - dg - 1, :, col]
-            send(part_i.at[away, col], dst, device(g=gg), ("bg", dg, k), ("bg", n_g - dg, k))
-
-    behind = min(BACK_AHEAD, links)
+            dst = from_g.at[n_g - dg - 1, 0, :, col]
+            send(part_i.at[away, col], dst, device(g=gg), ("bg", dg, 0, k), ("bg", n_g - dg, 0, k))
+
+    def early_f(k):
+        col = lcols(k)
+        for dx in range(n_x):
+            xx = (x + dx) % n_x
+            away = rows_of(xx * 2 + f2)
+            send(part_t.at[away, col], from_f.at[xx, :, col], device(f=f2), ("bf", dx, k), ("bf", dx, k))
+
+    def early_x(k):
+        col = lcols(k)
+        for dx in range(1, n_x):
+            xx = (x + dx) % n_x
+            away = rows_of(xx * 2 + f)
+            arrived(from_f.at[xx, :, col], ("bf", dx, k))
+            part_t[away, col] = part_t[away, col] + from_f[xx, :, col]
+            dst = from_x.at[n_x - dx - 1, 0:rows, col]
+            send(part_t.at[away, col], dst, device(x=xx), ("bx", dx, k), ("bx", n_x - dx, k))
+
+    def early_g(k):
+        col = lcols(k)
+        arrived(from_core.at[:, col], ("bc", k))
+        for dg in range(1, n_g):
+            gg = (g + dg) % n_g
+            for j in range(2):
+                at = ((y + j) % 2) * n_g + gg
+                away = rows_of(base + at)
+                part_i[away, col] = part_i[away, col] + from_core[rows_of(at), col]
+                dst = from_g.at[n_g - dg - 1, j, :, col]
+                send(part_i.at[away, col], dst, device(g=gg), ("bg", dg, j, k), ("bg", n_g - dg, j, k))
+        for j in range(2):
+            at = ((y + j) % 2) * n_g + g
+            keep = rows_of(base + at)
+            part_i[keep, col] = part_i[keep, col] + from_core[rows_of(at), col]
+
+    def early_y(k):
+        col = lcols(k)
+        away = rows_of(base + y2 * n_g + g)
+        total = part_i[away, col]
+        for dg in range(1, n_g):
+            arrived(from_g.at[dg - 1, 1, :, col], ("bg", dg, 1, k))
+            total = total + from_g[dg - 1, 1, :, col]
+        part_i[away, col] = total
+        send(part_i.at[away, col], from_y.at[0:rows, col], device(y=y2), ("by", k), ("by", k))
+
+    early = min(EARLY, links - 1)
     for k in range(chunks):
         partial_texts(k)
         for j in range(k * ratio, (k + 1) * ratio):
-            if j < behind:
+            if j < early:
+                early_f(j)
+            else:
                 send_x(j)
-        partial_images(k)
-        for j in range(k * ratio, (k + 1) * ratio):
-            send_core(j)
-            if j < behind:
-                send_y(j)
+        if k > 0:
+            partial_images(k - 1)
+            for j in range((k - 1) * ratio, k * ratio):
+                send_core(j)
+    partial_images(chunks - 1)
+    for j in range((chunks - 1) * ratio, links):
+        send_core(j)
+    for k in range(links):
+        if k < early:
+            early_g(k)
+        else:
+            send_y(k)
 
     row_lane = lax.broadcasted_iota(jnp.int32, (1, n_images), 1) // rows
     col_lane = lax.broadcasted_iota(jnp.int32, (1, n_texts), 1) // rows
@@ -400,13 +461,13 @@
         here = totals_i.at[own_i]
         send(here, here, to, ("ti", dg, dy, dc), ("ti",) + back)
 
-    for k in range(links):
+    for k in range(early, links):
         send_f(k)
-        if k + behind < links:
-            send_x(k + behind)
+        if k == links - 1:
+            for j in range(early):
+                early_x(j)
+                early_y(j)
         send_g(k)
-        if k + behind < links:
-            send_y(k + behind)
 
     for (dg, dy, dc), _, _ in image_peers:
         slot = image_slot((g + dg) % n_g, (y + dy) % 2, (core + dc) % 2)
@@ -416,16 +477,25 @@
         here = totals_t.at[own_t]
         send(here, here, to, ("tt", dx, df), ("tt",) + back)
 
-    for k in range(links):
-        col = lcols(k)
-        arrived(from_f.at[:, col], ("bf", k))
-        total = part_t[rows_of(x * 2 + f), col] + from_f[:, col]
-        text_grad_ref[:, col] = scale * (total - image_ref[:, col])
-        total = part_i[rows_of(own_i), col] + from_y[rows_of(g), col]
-        for dg in range(1, n_g):
-            arrived(from_g.at[dg - 1, :, col], ("bg", dg, k))
-            total = total + from_g[dg - 1, :, col]
-        image_grad_ref[:, col] = scale * (total - text_ref[:, col])
+    for k in [*range(early, links), *range(early)]:
+        col = lcols(k)
+        arrived(from_f.at[x, :, col], ("bf", 0, k))
+        total = part_t[rows_of(x * 2 + f), col] + from_f[x, :, col]
+        if k < early:
+            for dx in range(1, n_x):
+                arrived(from_x.at[dx - 1, 0:rows, col], ("bx", dx, k))
+                total = total + from_x[dx - 1, 0:rows, col]
+        text_grad_ref[:, col] = scale * (total - images[own_images, col])
+        total = part_i[rows_of(own_i), col]
+        for dg in range(1, n_g):
+            arrived(from_g.at[dg - 1, 0, :, col], ("bg", dg, 0, k))
+            total = total + from_g[dg - 1, 0, :, col]
+        if k < early:
+            arrived(from_y.at[0:rows, col], ("by", k))
+            total = total + from_y[0:rows, col]
+        else:
+            total = total + from_y[rows_of(g), col]
+        image_grad_ref[:, col] = scale * (total - texts[own_texts, col])
 
     for (dx, df), _, _ in text_peers:
         arrived(totals_t.at[text_slot((x + dx) % n_x, (f + df) % 2)], ("tt", dx, df))
@@ -444,9 +514,10 @@
     n_g, n_x = n_blk // 4, n_group // 2
     n_images, n_texts = rows * n_blk, rows * n_group
     links = emb // (LINK_WIDTH if width % LINK_WIDTH == 0 else width)
-    count = links * (n_g * 4 + n_x * 4 + 8) + 2 * (n_blk + n_group)
+    count = links * (n_g * 6 + n_x * 5 + 8) + 2 * (n_blk + n_group)
     vmem = pl.BlockSpec(memory_space=pltpu.VMEM)
     smem = pl.BlockSpec(memory_space=pltpu.SMEM)
+    hbm = pl.BlockSpec(memory_space=pl.ANY)
     image_grad, text_grad, mean_loss, scale_grad = pl.pallas_call(
         functools.partial(kernel, n_blk, n_group, width),
         out_shape=(
@@ -455,7 +526,7 @@
             jax.ShapeDtypeStruct((1,), F32),
             jax.ShapeDtypeStruct((1,), F32),
         ),
-        in_specs=[smem, vmem, vmem],
+        in_specs=[smem, hbm, hbm],
         out_specs=(vmem, vmem, smem, smem),
         scratch_shapes=[
             pltpu.VMEM((n_images, emb), F32),
@@ -474,15 +545,16 @@
             pltpu.VMEM((n_texts, emb), F32),
             pltpu.VMEM((n_images // 2, emb), F32),
             pltpu.VMEM((n_g * rows, emb), F32),
-            pltpu.VMEM((max(n_g - 1, 1), rows, emb), F32),
+            pltpu.VMEM((max(n_g - 1, 1), 2, rows, emb), F32),
             pltpu.VMEM((max(n_x - 1, 1), 2 * rows, emb), F32),
-            pltpu.VMEM((rows, emb), F32),
+            pltpu.VMEM((n_x, rows, emb), F32),
             pltpu.VMEM((n_blk, 1, n_images), F32),
             pltpu.VMEM((n_group, 1, n_texts), F32),
             pltpu.VMEM((n_blk, 1, 128), F32),
             pltpu.VMEM((n_group, 1, 128), F32),
             pltpu.SemaphoreType.DMA((count,)),
             pltpu.SemaphoreType.DMA((count,)),
+            pltpu.SemaphoreType.DMA((2,)),
         ],
         compiler_params=pltpu.CompilerParams(
             collective_id=0, has_side_effects=True, vmem_limit_bytes=56 * 1024 * 1024

time: 52 us -> 49.7 us (0.956)
  Pallas kernels: 44.6 us -> 42.3 us
    pallas_call x1, Pallas kernels: 44.6 us -> 42.3 us  [body(): pl.pallas_call(functools.partial(kernel, n_blk, n_group, width), out_shap...]
where the time goes in v3:
time: 49.7 us; the launch traced here: 49.5 us
  Pallas kernels  42.3 us (85%)
  between operations  4.81 us (10%)
  local copies, waits for them, and re-layouts  2.34 us (5%)
    pallas_call x1, Pallas kernels, body(): pl.pallas_call(functools.partial(kernel, n_blk, n_group, width), out_shap...  42.3 us
    unnamed x4, local copies, waits for them, and re-layouts  2.34 us

profile of v3, /device:TPU:0, one launch (start us, length us, event | category | flops | bytes accessed | tf_op | source)
XLA Modules:
  0.0 49.5 jit_solution(6323797823479332793)
XLA Ops:
  1.3 42.3 %contrastive.1 = (f32[64,768]{1,0:T(8,128)}, f32[64,768]{1,0:T(8,128)}, f32[1]{0:T(128)}, f32[1]{0:T(128)}) custom-call(f32[1]{0:T(128)S(6)} %copy.11.scale_ref, f32[64,768]{1,0:T(8,128)} %image_ref.1, f32[64,768]{1,0:T(8,128)} %text_ref.1), custom_call_target="tpu_custom_call" | custom-call | tf_op jit(solution)/shard_map/contrastive/pallas_call | solution.py:521
  43.6 0.0 copy-start
  43.6 1.7 %copy.12 = f32[64,768]{1,0:T(8,128)} copy(f32[64,768]{1,0:T(8,128)} %get-tuple-element.8) | data formatting | bytes 393216
  45.3 0.0 copy-done
  45.3 0.7 %copy.13 = f32[64,768]{1,0:T(8,128)} copy(f32[64,768]{1,0:T(8,128)S(1)} %copy-done) | data formatting | bytes 393216
Async XLA Ops:
  43.6 1.7 %copy-start = (f32[64,768]{1,0:T(8,128)S(1)}, f32[64,768]{1,0:T(8,128)}, u32[]{:S(2)}) copy-start(f32[64,768]{1,0:T(8,128)} %get-tuple-element.9) | copy-start | bytes 589828

commit v4 on v3

--- a/solution.py
+++ b/solution.py
@@ -15,7 +15,7 @@
 
 
 LINK_WIDTH = 256
-AHEAD = 2
+AHEAD = 3
 EARLY = 1
 
 
@@ -190,6 +190,9 @@
         begin(k)
 
     def relay(k):
+        at = block(images, image_slot(y=y2), k)
+        arrived(at, ("iy", 0, k))
+        send(at, at, device(core=core2), ("ic", 0, 1, k), ("ic", 0, 1, k))
         for dg in range(1, n_g):
             at = block(images, image_slot(g=(g + dg) % n_g), k)
             arrived(at, ("ig", dg, k))
@@ -199,9 +202,6 @@
         arrived(at, ("tf", k))
         for dx in range(1, n_x):
             send(at, at, device(x=(x + dx) % n_x), ("tx", dx, 1, k), ("tx", n_x - dx, 1, k))
-        at = block(images, image_slot(y=y2), k)
-        arrived(at, ("iy", 0, k))
-        send(at, at, device(core=core2), ("ic", 0, 1, k), ("ic", 0, 1, k))
 
     def relay_last(k):
         for dg in range(1, n_g):

time: 49.7 us -> 49.4 us (level)
  no operation moved by 1% of the time
where the time goes in v4:
time: 49.4 us; the launch traced here: 49.2 us
  Pallas kernels  42.1 us (85%)
  between operations  4.81 us (10%)
  local copies, waits for them, and re-layouts  2.34 us (5%)
    pallas_call x1, Pallas kernels, body(): pl.pallas_call(functools.partial(kernel, n_blk, n_group, width), out_shap...  42.1 us
    unnamed x4, local copies, waits for them, and re-layouts  2.34 us

profile of v4, /device:TPU:0, one launch (start us, length us, event | category | flops | bytes accessed | tf_op | source)
XLA Modules:
  0.0 49.2 jit_solution(8716540482692526777)
XLA Ops:
  1.3 42.1 %contrastive.1 = (f32[64,768]{1,0:T(8,128)}, f32[64,768]{1,0:T(8,128)}, f32[1]{0:T(128)}, f32[1]{0:T(128)}) custom-call(f32[1]{0:T(128)S(6)} %copy.11.scale_ref, f32[64,768]{1,0:T(8,128)} %image_ref.1, f32[64,768]{1,0:T(8,128)} %text_ref.1), custom_call_target="tpu_custom_call" | custom-call | tf_op jit(solution)/shard_map/contrastive/pallas_call | solution.py:521
  43.4 0.0 copy-start
  43.4 1.7 %copy.12 = f32[64,768]{1,0:T(8,128)} copy(f32[64,768]{1,0:T(8,128)} %get-tuple-element.8) | data formatting | bytes 393216
  45.0 0.0 copy-done
  45.0 0.7 %copy.13 = f32[64,768]{1,0:T(8,128)} copy(f32[64,768]{1,0:T(8,128)S(1)} %copy-done) | data formatting | bytes 393216
Async XLA Ops:
  43.4 1.7 %copy-start = (f32[64,768]{1,0:T(8,128)S(1)}, f32[64,768]{1,0:T(8,128)}, u32[]{:S(2)}) copy-start(f32[64,768]{1,0:T(8,128)} %get-tuple-element.9) | copy-start | bytes 589828
